TPU v7x, 512 devices: a whole 4x4x16 slice. The times are simulated.
512 devices in a mesh: pair: 2 (over core), latent: 32 (over x, z_lo), tok: 8 (over y, z_hi).
Axes of the slice: x: 4, y: 4, z: 16 (z_hi: 2, z_lo: 8; z = z_hi * 8 + z_lo), core: 2. Of those that a mesh axis runs over, the one named last changes fastest.
Arguments:
- activations: bfloat16 [2, 512, 3584], P('pair', 'tok'), may hold values from -6 to 6
- enc_weight: bfloat16 [2, 3584, 65536], P('pair', None, ('latent', 'tok')), may hold values from -0.0625 to 0.0625
- enc_bias: float32 [65536], P(('latent', 'tok')), may hold values from -3 to 3
- thresholds: int32 [65536], P(('latent', 'tok')), may hold values from 1 to 4
- dec_weight: bfloat16 [2, 65536, 3584], P('pair', 'latent', 'tok'), may hold values from -0.0234375 to 0.0234375
- dec_bias: float32 [2, 3584], P('pair', 'tok'), may hold values from -3 to 3
Outputs:
- recon: bfloat16 [2, 512, 3584], P('pair', 'latent', 'tok')
- token_loss: float32 [512], P('latent')
- scaling: float32 [2, 65536], P('pair', ('latent', 'tok'))
All inputs are finite; a program needn't handle non-finite values.
Results may differ from a plain program's by a relative error of at most 0.017.
Values may be sent and summed in bfloat16 or wider, within the bound.
No kernel may reach another device: no remote copies, remote signals or barrier semaphores. Data moves between devices by JAX's collectives and lax.ppermute only.
A program may use at most 64 MiB of HBM per device.

v0:
```python
import jax
import jax.numpy as jnp
from jax import lax
from jax.sharding import PartitionSpec as P

D = 3584
smooth_width = 0.1
penalty = 0.0001
tiny_term = 1e-06


def body(activations, enc_weight, enc_bias, thresholds, dec_weight, dec_bias):
    gathered = lax.all_gather(activations[0], "tok", axis=0, tiled=True)
    partial_value = jnp.dot(gathered, enc_weight[0], preferred_element_type=jnp.float32)
    thresh_level = thresholds.astype(jnp.float32) * 0.25
    shifted = lax.psum(partial_value, "pair") + enc_bias
    local_feats = (shifted * jax.nn.sigmoid((shifted - thresh_level) / smooth_width)).astype(
        jnp.bfloat16
    )
    block_feats = lax.all_gather(local_feats, "tok", axis=1, tiled=True)
    tok_index = lax.axis_index("tok")
    lat_index = lax.axis_index("latent")
    dec_block = dec_weight[0]
    slice_width = dec_block.shape[1]
    own_count = enc_weight.shape[2]
    tokens_all = block_feats.shape[0]
    row_count = tokens_all // lax.axis_size("latent")
    act_slice = lax.dynamic_slice_in_dim(gathered, tok_index * slice_width, slice_width, 1)
    inner_prod = lax.dot_general(
        block_feats, act_slice, (((0,), (0,)), ((), ())), preferred_element_type=jnp.float32
    )
    dec_wide = dec_block.astype(jnp.float32)
    num_part = jnp.sum(inner_prod * dec_wide, axis=1)
    nsq_part = jnp.sum(dec_wide * dec_wide, axis=1)
    num_all, nsq_all = lax.psum((num_part, nsq_part), "tok")
    norm_vals = jnp.sqrt(nsq_all)
    own_cols = lax.dynamic_slice_in_dim(block_feats, tok_index * own_count, own_count, 1).astype(
        jnp.float32
    )
    mean_sq = jnp.mean(own_cols * own_cols, axis=0)
    num_own = lax.dynamic_slice_in_dim(num_all, tok_index * own_count, own_count, 0) / tokens_all
    nsq_own = lax.dynamic_slice_in_dim(nsq_all, tok_index * own_count, own_count, 0)
    scaling = num_own / (nsq_own * mean_sq + tiny_term)
    recon_part = lax.psum_scatter(
        jnp.dot(block_feats, dec_block, preferred_element_type=jnp.float32),
        "latent",
        scatter_dimension=0,
        tiled=True,
    )
    recon_vals = recon_part + dec_bias[0]
    act_own = lax.dynamic_slice_in_dim(act_slice, lat_index * row_count, row_count, 0).astype(
        jnp.float32
    )
    residue = act_own - recon_vals
    sq_error = jnp.sum(residue * residue, axis=1)
    sparse = jnp.sum(block_feats.astype(jnp.float32) * norm_vals, axis=1)
    sparse_term = penalty * sparse / lax.axis_size("tok")
    own_terms = lax.dynamic_slice_in_dim(
        sparse_term, lat_index * row_count, row_count, 0
    ) + sq_error / (2.0 * D)
    loss_terms = lax.dynamic_update_slice_in_dim(sparse_term, own_terms, lat_index * row_count, 0)
    summed = lax.psum(loss_terms, ("pair", "latent", "tok"))
    token_loss = lax.dynamic_slice_in_dim(summed, lat_index * row_count, row_count, 0)
    return (recon_vals.astype(jnp.bfloat16)[None], token_loss, scaling[None])


def solution(mesh):
    return jax.shard_map(
        body,
        mesh=mesh,
        in_specs=(
            P("pair", "tok", None),
            P("pair", None, ("latent", "tok")),
            P(("latent", "tok")),
            P(("latent", "tok")),
            P("pair", "latent", "tok"),
            P("pair", "tok"),
        ),
        out_specs=(P("pair", "latent", "tok"), P("latent"), P("pair", ("latent", "tok"))),
        check_vma=False,
    )
```

profile of v0, /device:TPU:1, one launch (start us, length us, event | category | flops | bytes accessed | tf_op | source)
XLA Modules:
  0.0 686.3 jit_solution(3793005959864992193)
XLA Ops:
  7.2 0.0 copy-start
  7.2 0.0 all-gather.6.cloned.1.call-start
  7.2 0.7 all-gather.6.cloned.1.call-update
  7.9 0.0 copy-start.3
  7.9 0.0 copy-start.2
  7.9 0.0 all-reduce.3.cloned.1.call-start
  8.0 168.3 %all-gather.6.cloned.1.call-done = bf16[1,512,3584]{2,1,0:T(8,128)(2,1)} async-done(((bf16[1,64,3584]{2,1,0:T(8,128)(2,1)}), bf16[1,512,3584]{2,1,0:T(8,128)(2,1)}) %all-gather.6.cloned.1.call-update) | async-done | bytes 3670032 | tf_op jit(solution)/shard_map/all_gather | solution.py:13
  176.3 0.0 copy-done
  176.3 3.9 fusion.2
  180.3 0.0 all-reduce.3.cloned.1.call-update
  180.3 0.0 all-gather.4.cloned.1.call-start
  180.3 0.0 copy-done.3
  180.4 35.7 %all-reduce.3.cloned.1.call-done = f32[512,256]{1,0:T(8,128)} async-done(((f32[512,256]{1,0:T(8,128)}), f32[512,256]{1,0:T(8,128)}) %all-reduce.3.cloned.1.call-update) | async-done | bytes 524304 | tf_op jit(solution)/shard_map/psum | solution.py:16
  216.1 0.0 copy-done.2
  216.1 1.9 multiply_convert_fusion
  218.0 0.0 all-gather.4.cloned.1.call-update
  218.0 0.0 reduce-scatter.2.cloned.1.call-start
  218.1 118.3 %all-gather.4.cloned.1.call-done = bf16[512,2048]{1,0:T(8,128)(2,1)} async-done(((bf16[512,256]{1,0:T(8,128)(2,1)}), bf16[512,2048]{1,0:T(8,128)(2,1)}) %all-gather.4.cloned.1.call-update) | async-done | bytes 2097168 | tf_op jit(solution)/shard_map/all_gather | solution.py:20
  336.4 4.4 fusion.4
  340.8 0.0 reduce-scatter.2.cloned.1.call-update
  340.8 1.9 fusion
  342.7 3.7 fusion.1
  346.4 0.0 copy-start.1
  346.4 58.9 %all-reduce = (f32[2048]{0:T(1024)S(1)}, f32[2048]{0:T(1024)S(1)}) all-reduce(f32[2048]{0:T(1024)S(1)} %fusion, f32[2048]{0:T(1024)S(1)} %fusion.1), channel_id=1, replica_groups=mesh['pair'=2,'latent'=32,'tok'=8] {'tok'}, use_global_device_ids=true, to_apply=%region_3.0 | all-reduce | flops 4096 | bytes 32768 | tf_op jit(solution)/shard_map/psum | solution.py:35
  405.2 1.0 multiply_reduce_fusion.1
  406.3 0.6 add_divide_fusion
  406.9 2.1 multiply_reduce_fusion
  409.0 144.2 %reduce-scatter.2.cloned.1.call-done = f32[16,448]{1,0:T(8,128)} async-done(((f32[512,448]{1,0:T(8,128)}), f32[16,448]{1,0:T(8,128)}) %reduce-scatter.2.cloned.1.call-update) | async-done | bytes 28688 | tf_op jit(solution)/shard_map/reduce_scatter | solution.py:44
  553.3 0.0 copy-done.1
  553.3 1.5 fusion.10
  554.8 0.2 add_dynamic-update-slice_fusion
  554.9 124.3 %psum.30 = f32[512]{0:T(512)S(1)} all-reduce(f32[512]{0:T(512)S(1)} %add_dynamic-update-slice_fusion), channel_id=1, replica_groups=mesh['pair'=2,'latent'=32,'tok'=8] {'pair','latent','tok'}, use_global_device_ids=true, to_apply=%region_6.0 | all-reduce | flops 512 | bytes 4096 | tf_op jit(solution)/shard_map/psum | solution.py:62
  679.2 0.6 dynamic_slice.23
  (3 shorter events, 0.0 us)
Async XLA Ops:
  7.2 169.2 %copy-start = (bf16[1,3584,256]{2,1,0:T(8,128)(2,1)S(1)}, bf16[1,3584,256]{2,1,0:T(8,128)(2,1)}, u32[]{:S(2)}) copy-start(bf16[1,3584,256]{2,1,0:T(8,128)(2,1)} %param.7) | copy-start | bytes 5505028
  7.2 169.1 %all-gather.6.cloned.1.call-start = ((), (), s32[]{:S(2)}) async-start(), calls=%async_computation.4 | async-start | bytes 4128768 | tf_op jit(solution)/shard_map/all_gather | solution.py:13
  7.9 172.4 %copy-start.3 = (s32[256]{0:T(256)S(1)}, s32[256]{0:T(256)}, u32[]{:S(2)}) copy-start(s32[256]{0:T(256)} %param.9) | copy-start | bytes 3076
  7.9 208.2 %copy-start.2 = (f32[256]{0:T(256)S(1)}, f32[256]{0:T(256)}, u32[]{:S(2)}) copy-start(f32[256]{0:T(256)} %param.8) | copy-start | bytes 3076
  7.9 208.2 %all-reduce.3.cloned.1.call-start = ((), (), s32[]{:S(2)}) async-start(), calls=%async_computation.1 | async-start | bytes 1048576 | tf_op jit(solution)/shard_map/psum | solution.py:16
  180.3 156.1 %all-gather.4.cloned.1.call-start = ((), (), s32[]{:S(2)}) async-start(), calls=%async_computation.2 | async-start | bytes 2359296 | tf_op jit(solution)/shard_map/all_gather | solution.py:20
  218.0 335.2 %reduce-scatter.2.cloned.1.call-start = ((), (), s32[]{:S(2)}) async-start(), calls=%async_computation.3 | async-start | bytes 1081344 | tf_op jit(solution)/shard_map/reduce_scatter | solution.py:44
  346.4 206.9 %copy-start.1 = (f32[1,448]{1,0:T(1,128)S(1)}, f32[1,448]{1,0:T(1,128)}, u32[]{:S(2)}) copy-start(f32[1,448]{1,0:T(1,128)} %param.11) | copy-start | bytes 5380
Sparse Core Ops, SparseCore 0:
  11.2 165.0 all-gather.5
  180.4 35.6 all-reduce.2
  219.6 116.7 all-gather.3
  340.9 212.3 reduce-scatter.1
where the time goes:
time: 687 us; the launch traced here: 686 us
  waiting for transfers between devices  467 us (68%)
  blocking collectives  183 us (27%)
  between operations  13.8 us (2%)
  matrix products  12 us (2%)
  other arithmetic  9.24 us (1%)
    all_gather x1, waiting for transfers between devices, body(): gathered = lax.all_gather(activations[0], 'tok', axis=0, tiled=True)  168 us
    reduce_scatter x1, waiting for transfers between devices, body(): lax.psum_scatter(jnp.dot(block_feats, dec_block, preferred_element_type=j...  144 us
    psum x1, blocking collectives, body(): summed = lax.psum(loss_terms, ('pair', 'latent', 'tok'))  124 us
    all_gather x1, waiting for transfers between devices, body(): block_feats = lax.all_gather(local_feats, 'tok', axis=1, tiled=True)  118 us
    psum x1, blocking collectives, body(): num_all, nsq_all = lax.psum((num_part, nsq_part), 'tok')  58.9 us
    psum x1, waiting for transfers between devices, body(): shifted = lax.psum(partial_value, 'pair') + enc_bias  35.7 us
  transfers between devices with their start and end apart: 4, of which 4 were waited for; matrix products, arithmetic and copies ran while one was open for 1% of the time, Pallas kernels for 0%

commit v1 on v0

--- a/solution.py
+++ b/solution.py
@@ -13,7 +13,7 @@
     gathered = lax.all_gather(activations[0], "tok", axis=0, tiled=True)
     partial_value = jnp.dot(gathered, enc_weight[0], preferred_element_type=jnp.float32)
     thresh_level = thresholds.astype(jnp.float32) * 0.25
-    shifted = lax.psum(partial_value, "pair") + enc_bias
+    shifted = jnp.sum(lax.all_gather(partial_value, "pair"), axis=0) + enc_bias
     local_feats = (shifted * jax.nn.sigmoid((shifted - thresh_level) / smooth_width)).astype(
         jnp.bfloat16
     )

time: 687 us -> 666 us (0.969)
  waiting for transfers between devices: 467 us -> 446 us
    psum x1 -> x0, waiting for transfers between devices: 35.7 us -> none  [body(): shifted = lax.psum(partial_value, 'pair') + enc_bias]
    all_gather x0 -> x1, waiting for transfers between devices: none -> 15.4 us  [body(): shifted = jnp.sum(lax.all_gather(partial_value, 'pair'), axis=0) + enc_bias]
where the time goes in v1:
time: 666 us; the launch traced here: 665 us
  waiting for transfers between devices  446 us (67%)
  blocking collectives  184 us (28%)
  between operations  13.8 us (2%)
  matrix products  12 us (2%)
  other arithmetic  9.58 us (1%)
    all_gather x1, waiting for transfers between devices, body(): gathered = lax.all_gather(activations[0], 'tok', axis=0, tiled=True)  168 us
    reduce_scatter x1, waiting for transfers between devices, body(): lax.psum_scatter(jnp.dot(block_feats, dec_block, preferred_element_type=j...  144 us
    psum x1, blocking collectives, body(): summed = lax.psum(loss_terms, ('pair', 'latent', 'tok'))  125 us
    all_gather x1, waiting for transfers between devices, body(): block_feats = lax.all_gather(local_feats, 'tok', axis=1, tiled=True)  117 us
    psum x1, blocking collectives, body(): num_all, nsq_all = lax.psum((num_part, nsq_part), 'tok')  58.9 us
    all_gather x1, waiting for transfers between devices, body(): shifted = jnp.sum(lax.all_gather(partial_value, 'pair'), axis=0) + enc_bias  15.4 us
  transfers between devices with their start and end apart: 4, of which 4 were waited for; matrix products, arithmetic and copies ran while one was open for 1% of the time, Pallas kernels for 0%

profile of v1, /device:TPU:1, one launch (start us, length us, event | category | flops | bytes accessed | tf_op | source)
XLA Modules:
  0.0 665.5 jit_solution(16582062026901741808)
XLA Ops:
  7.2 0.0 copy-start
  7.2 0.0 all-gather.8.cloned.1.call-start
  7.2 0.7 all-gather.8.cloned.1.call-update
  7.9 0.0 copy-start.3
  7.9 0.0 all-gather.10.cloned.1.call-start
  8.0 168.4 %all-gather.8.cloned.1.call-done = bf16[1,512,3584]{2,1,0:T(8,128)(2,1)} async-done(((bf16[1,64,3584]{2,1,0:T(8,128)(2,1)}), bf16[1,512,3584]{2,1,0:T(8,128)(2,1)}) %all-gather.8.cloned.1.call-update) | async-done | bytes 3670032 | tf_op jit(solution)/shard_map/all_gather | solution.py:13
  176.3 0.0 copy-done
  176.3 4.0 fusion.2
  180.3 0.0 copy-start.2
  180.3 0.0 all-gather.10.cloned.1.call-update
  180.3 0.0 all-gather.6.cloned.1.call-start
  180.4 0.0 copy-done.3
  180.4 15.4 %all-gather.10.cloned.1.call-done = f32[1024,256]{1,0:T(8,128)} async-done(((f32[512,256]{1,0:T(8,128)}), f32[1024,256]{1,0:T(8,128)}) %all-gather.10.cloned.1.call-update) | async-done | bytes 1048592 | tf_op jit(solution)/shard_map/all_gather | solution.py:16
  195.8 1.4 reduce_sum.54
  197.2 0.0 copy-done.2
  197.2 0.9 multiply_convert_fusion
  198.1 0.0 all-gather.6.cloned.1.call-update
  198.1 0.0 reduce-scatter.2.cloned.1.call-start
  198.1 117.5 %all-gather.6.cloned.1.call-done = bf16[512,2048]{1,0:T(8,128)(2,1)} async-done(((bf16[512,256]{1,0:T(8,128)(2,1)}), bf16[512,2048]{1,0:T(8,128)(2,1)}) %all-gather.6.cloned.1.call-update) | async-done | bytes 2097168 | tf_op jit(solution)/shard_map/all_gather | solution.py:20
  315.6 4.4 fusion.4
  320.0 0.0 reduce-scatter.2.cloned.1.call-update
  320.1 1.9 fusion
  322.0 3.7 fusion.1
  325.6 0.0 copy-start.1
  325.6 58.9 %all-reduce = (f32[2048]{0:T(1024)S(1)}, f32[2048]{0:T(1024)S(1)}) all-reduce(f32[2048]{0:T(1024)S(1)} %fusion, f32[2048]{0:T(1024)S(1)} %fusion.1), channel_id=1, replica_groups=mesh['pair'=2,'latent'=32,'tok'=8] {'tok'}, use_global_device_ids=true, to_apply=%region_3.0 | all-reduce | flops 4096 | bytes 32768 | tf_op jit(solution)/shard_map/psum | solution.py:35
  384.6 1.0 multiply_reduce_fusion.1
  385.6 0.6 add_divide_fusion
  386.2 2.1 multiply_reduce_fusion
  388.3 143.7 %reduce-scatter.2.cloned.1.call-done = f32[16,448]{1,0:T(8,128)} async-done(((f32[512,448]{1,0:T(8,128)}), f32[16,448]{1,0:T(8,128)}) %reduce-scatter.2.cloned.1.call-update) | async-done | bytes 28688 | tf_op jit(solution)/shard_map/reduce_scatter | solution.py:44
  532.1 0.0 copy-done.1
  532.1 1.5 fusion.10
  533.6 0.2 add_dynamic-update-slice_fusion
  533.7 124.6 %psum.22 = f32[512]{0:T(512)S(1)} all-reduce(f32[512]{0:T(512)S(1)} %add_dynamic-update-slice_fusion), channel_id=1, replica_groups=mesh['pair'=2,'latent'=32,'tok'=8] {'pair','latent','tok'}, use_global_device_ids=true, to_apply=%region_6.0 | all-reduce | flops 512 | bytes 4096 | tf_op jit(solution)/shard_map/psum | solution.py:62
  658.4 0.6 dynamic_slice.23
  (3 shorter events, 0.0 us)
Async XLA Ops:
  7.2 169.2 %copy-start = (bf16[1,3584,256]{2,1,0:T(8,128)(2,1)S(1)}, bf16[1,3584,256]{2,1,0:T(8,128)(2,1)}, u32[]{:S(2)}) copy-start(bf16[1,3584,256]{2,1,0:T(8,128)(2,1)} %param.7) | copy-start | bytes 5505028
  7.2 169.1 %all-gather.8.cloned.1.call-start = ((), (), s32[]{:S(2)}) async-start(), calls=%async_computation.3 | async-start | bytes 4128768 | tf_op jit(solution)/shard_map/all_gather | solution.py:13
  7.9 172.5 %copy-start.3 = (s32[256]{0:T(256)S(1)}, s32[256]{0:T(256)}, u32[]{:S(2)}) copy-start(s32[256]{0:T(256)} %param.9) | copy-start | bytes 3076
  7.9 187.9 %all-gather.10.cloned.1.call-start = ((), (), s32[]{:S(2)}) async-start(), calls=%async_computation.4 | async-start | bytes 1572864 | tf_op jit(solution)/shard_map/all_gather | solution.py:16
  180.3 16.9 %copy-start.2 = (f32[256]{0:T(256)S(1)}, f32[256]{0:T(256)}, u32[]{:S(2)}) copy-start(f32[256]{0:T(256)} %param.8) | copy-start | bytes 3076
  180.3 135.3 %all-gather.6.cloned.1.call-start = ((), (), s32[]{:S(2)}) async-start(), calls=%async_computation.1 | async-start | bytes 2359296 | tf_op jit(solution)/shard_map/all_gather | solution.py:20
  198.1 334.0 %reduce-scatter.2.cloned.1.call-start = ((), (), s32[]{:S(2)}) async-start(), calls=%async_computation.2 | async-start | bytes 1081344 | tf_op jit(solution)/shard_map/reduce_scatter | solution.py:44
  325.6 206.4 %copy-start.1 = (f32[1,448]{1,0:T(1,128)S(1)}, f32[1,448]{1,0:T(1,128)}, u32[]{:S(2)}) copy-start(f32[1,448]{1,0:T(1,128)} %param.11) | copy-start | bytes 5380
Sparse Core Ops, SparseCore 0:
  11.2 165.0 all-gather.7
  180.4 15.3 all-gather.9
  198.9 116.7 all-gather.5
  320.2 211.8 reduce-scatter.1
